TPU v7x, 32 devices: a whole 2x2x4 slice. The times are simulated.
32 devices in a mesh: row: 4 (over y, x), col: 8 (over z, core).
Axes of the slice: x: 2, y: 2, z: 4, core: 2. Of those that a mesh axis runs over, the one named last changes fastest.
Arguments:
- tokens: bfloat16 [4096, 2880], P(('col', 'row')), may hold values from -6 to 6
- seg_ids: int32 [4096], P(('col', 'row')), may hold values from 0 to 3, never falling along the last dimension, each value on 1 to 2048 neighbouring positions
- norm_gain: float32 [2880], replicated, may hold values from 0.1 to 1.9
- query_weight: bfloat16 [2880, 4096], P('col', 'row'), may hold values from -4.5839394 to 4.5839394
- kv_weight: bfloat16 [2880, 1024], P('col', 'row'), may hold values from -0.1118034 to 0.1118034
- out_weight: bfloat16 [4096, 2880], P('row', 'col'), may hold values from -0.09375 to 0.09375
- sinks: float32 [64], P('row'), may hold values from 1 to 6
- moe_gain: float32 [2880], replicated, may hold values from 0.1 to 1.9
- routes: int32 [4096, 4], P(('col', 'row')), may hold values from 0 to 63, all different within a row; in each aligned block of 128 rows (0 to 127, 128 to 255, ...) at most 9 rows name the same one
- route_weights: float32 [4096, 4], P(('col', 'row')), may hold values from 0.05 to 0.5
- expert_in: bfloat16 [128, 2880, 1536], P(('row', 'col')), may hold values from -0.109375 to 0.109375
- expert_out: bfloat16 [128, 768, 2880], P(('row', 'col')), may hold values from -0.21875 to 0.21875
Outputs:
- mixed: bfloat16 [4096, 2880], P(('col', 'row'))
- kv_cache: bfloat16 [4096, 1024], P('col', 'row')
Inputs may be any that keep to these rules, and one draw needn't show every extreme that they name: `seg_ids`: never falling; each prompt has 1 to 2048 tokens, one exactly 2048. `routes`: each row names 4 different experts; among the 128 rows of one device no expert is named more than 9 times, and on some device one is named exactly 9 times.
All inputs are finite; a program needn't handle non-finite values.
Results may differ from a plain program's by a relative error of at most 0.012.
Values may be sent and summed in bfloat16 or wider, within the bound.
No kernel may reach another device: no remote copies, remote signals or barrier semaphores. Data moves between devices by JAX's collectives and lax.ppermute only.
A program may use at most 128 MiB of HBM per device.

v0:
```python
import math

import jax
import jax.numpy as jnp
from jax import lax
from jax.experimental import pallas as pl
from jax.experimental.pallas import tpu as pltpu
from jax.sharding import PartitionSpec as P

HD = 64
WIN = 128
EXPERTS = 64
TOP = 4
CAP = 9


eps_norm = 1e-05
theta_base = 150000.0
glu_alpha = 1.702
masked_score = -1e30


def from_behind(value, axis, steps):
    count = lax.axis_size(axis)
    first, last = (max(0, -steps), min(count, count - steps))
    return lax.ppermute(value, axis, [(source, source + steps) for source in range(first, last)])


def rms_scale(values_in, gain_vec):
    widened = values_in.astype(jnp.float32)
    return (
        widened
        * lax.rsqrt(jnp.mean(widened * widened, axis=-1, keepdims=True) + eps_norm)
        * gain_vec
    )


def rotate(values_in, positions):
    half_dim = values_in.shape[-1] // 2
    frequency = jnp.exp(
        jnp.arange(half_dim, dtype=jnp.float32)
        * (-2.0 * math.log(theta_base) / values_in.shape[-1])
    )
    angles = positions.astype(jnp.float32)[:, None] * frequency[None, :]
    cosine = jnp.cos(angles)[:, None, :]
    sine = jnp.sin(angles)[:, None, :]
    first_half = values_in[..., :half_dim]
    second_half = values_in[..., half_dim:]
    return jnp.concatenate(
        [first_half * cosine - second_half * sine, second_half * cosine + first_half * sine],
        axis=-1,
    )


def attend_tile(
    query_tile, key_tile, value_tile, query_seg, key_seg, query_pos, key_pos, sink_grid
):
    scores = jnp.einsum(
        "qkgd,lkd->kgql", query_tile, key_tile, preferred_element_type=jnp.float32
    ) * query_tile.shape[-1] ** (-0.5)
    distance = query_pos[:, None] - key_pos[None, :]
    allowed = (
        (query_seg[:, None] == key_seg[None, :])
        & (distance >= 0)
        & (distance < WIN)
        & (key_pos[None, :] >= 0)
    )
    scores = jnp.where(allowed[None, None], scores, masked_score)
    sink_col = sink_grid[:, :, None]
    ceiling = jnp.maximum(jnp.max(scores, axis=-1), sink_col)
    expo = jnp.exp(scores - ceiling[..., None])
    denom = jnp.sum(expo, axis=-1) + jnp.exp(sink_col - ceiling)
    probs = (expo / denom[..., None]).astype(jnp.bfloat16)
    return jnp.einsum(
        "kgql,lkd->qkgd", probs, value_tile, preferred_element_type=jnp.float32
    ).astype(jnp.bfloat16)


LANES = 128
MAIN = CAP - 1
FULL_VMEM = 56 * 1024 * 1024


def up_to(count, multiple):
    return -(-count // multiple) * multiple


def swap_rows(value, distance):
    count = lax.axis_size("row")
    return lax.ppermute(value, "row", [(place, place ^ distance) for place in range(count)])


def whole_spec():
    return pl.BlockSpec(memory_space=pltpu.VMEM)


def dot32(left, right):
    return jnp.dot(left, right, preferred_element_type=jnp.float32)


def piece_widths(feature_dim):
    piece = up_to(-(-feature_dim // MAIN), LANES)
    return up_to(feature_dim, LANES), piece


def as_bf16(condition):
    return jnp.where(condition, 1.0, 0.0).astype(jnp.bfloat16)


def hidden_kernel(counts, share, *refs):
    tokens_ref, gain_ref = refs[:2]
    part_refs, (hidden_ref, normed_ref) = refs[2:-2], refs[-2:]
    at = 0
    sums = []
    for count in counts:
        total = part_refs[at][...].astype(jnp.float32)
        for other in range(1, count):
            total = total + part_refs[at + other][...].astype(jnp.float32)
        at += count
        sums.append(total)
    pieces = []
    for block in range(tokens_ref.shape[1] // sum(share)):
        for size, total in zip(share, sums):
            pieces.append(total[:, block * size : (block + 1) * size])
    hidden = tokens_ref[...].astype(jnp.float32) + jnp.concatenate(pieces, axis=1)
    hidden_ref[...] = hidden
    scale = lax.rsqrt(jnp.mean(hidden * hidden, axis=-1, keepdims=True) + eps_norm)
    normed_ref[...] = (hidden * scale * gain_ref[...]).astype(jnp.bfloat16)


def hidden_and_norm(tokens, gain, parts, share):
    flat = [part for group in parts for part in group]
    return pl.pallas_call(
        lambda *refs: hidden_kernel(tuple(len(group) for group in parts), share, *refs),
        out_shape=[
            jax.ShapeDtypeStruct(tokens.shape, jnp.float32),
            jax.ShapeDtypeStruct(tokens.shape, jnp.bfloat16),
        ],
        in_specs=[whole_spec()] * (2 + len(flat)),
        out_specs=[whole_spec()] * 2,
        compiler_params=pltpu.CompilerParams(vmem_limit_bytes=FULL_VMEM),
    )(tokens, gain, *flat)


def pack_kernel(rows_ref, code_ref, out_ref, padded_ref):
    feature_dim = rows_ref.shape[1]
    main_width, piece = piece_widths(feature_dim)
    padded_ref[...] = jnp.zeros_like(padded_ref)
    padded_ref[:, :feature_dim] = rows_ref[...]
    for group in range(code_ref.shape[0]):
        codes = code_ref[group]
        slot = lax.broadcasted_iota(jnp.int32, codes.shape, 0) % MAIN
        fold = (codes.shape[0] // MAIN, MAIN, -1)
        out_ref[:, group, :, :main_width] = (
            dot32(as_bf16(codes == slot), padded_ref[:, :main_width])
            .reshape(fold)
            .astype(jnp.bfloat16)
        )
        tail = jnp.zeros((codes.shape[0], piece), jnp.float32)
        for j in range(MAIN):
            tail = tail + dot32(
                as_bf16((codes == MAIN) & (slot == j)), padded_ref[:, j * piece : (j + 1) * piece]
            )
        out_ref[:, group, :, main_width:] = tail.reshape(fold).astype(jnp.bfloat16)


def pack(rows, codes):
    main_width, piece = piece_widths(rows.shape[1])
    return pl.pallas_call(
        pack_kernel,
        out_shape=jax.ShapeDtypeStruct(
            (codes.shape[1] // MAIN, codes.shape[0], MAIN, main_width + piece), jnp.bfloat16
        ),
        in_specs=[whole_spec()] * 2,
        out_specs=whole_spec(),
        scratch_shapes=[pltpu.VMEM((rows.shape[0], MAIN * piece), jnp.bfloat16)],
        compiler_params=pltpu.CompilerParams(vmem_limit_bytes=FULL_VMEM),
    )(rows, codes)


def expert_kernel(feature_dim, x_ref, gate_ref, up_ref, down_ref, y_ref, x_all, total):
    main_width, piece = piece_widths(feature_dim)
    senders = x_ref.shape[0]
    main_rows = senders * MAIN
    step = pl.program_id(1) * pl.num_programs(2) + pl.program_id(2)
    last = pl.num_programs(1) * pl.num_programs(2) - 1

    @pl.when(step == 0)
    def _():
        x_all[:main_rows, :main_width] = x_ref[:, 0, :, :main_width].reshape(main_rows, main_width)
        row = lax.broadcasted_iota(jnp.int32, (senders, main_rows), 0)
        col = lax.broadcasted_iota(jnp.int32, (senders, main_rows), 1)
        tail = x_ref[:, 0, :, main_width:].reshape(main_rows, piece)
        for j in range(MAIN):
            x_all[main_rows:, j * piece : (j + 1) * piece] = dot32(
                as_bf16(col == row * MAIN + j), tail
            ).astype(jnp.bfloat16)

    x = x_all[:, :feature_dim]
    gate_part = dot32(x, gate_ref[0])
    up_part = dot32(x, up_ref[0])
    hidden_act = (gate_part * jax.nn.sigmoid(glu_alpha * gate_part) * (up_part + 1.0)).astype(
        jnp.bfloat16
    )
    product = lax.dot_general(
        hidden_act, down_ref[0], (((1,), (1,)), ((), ())), preferred_element_type=jnp.float32
    )

    @pl.when(step == 0)
    def _():
        total[...] = product

    @pl.when(step > 0)
    def _():
        total[...] += product

    @pl.when(step == last)
    def _():
        y_ref[:, 0, :, feature_dim:main_width] = jnp.zeros(
            (senders, MAIN, main_width - feature_dim), jnp.bfloat16
        )
        y_ref[:, 0, :, :feature_dim] = (
            total[:main_rows].reshape(senders, MAIN, feature_dim).astype(jnp.bfloat16)
        )
        x_all[main_rows:, :] = jnp.zeros((senders, MAIN * piece), jnp.bfloat16)
        x_all[main_rows:, :feature_dim] = total[main_rows:].astype(jnp.bfloat16)
        row = lax.broadcasted_iota(jnp.int32, (main_rows, senders), 0)
        col = lax.broadcasted_iota(jnp.int32, (main_rows, senders), 1)
        tail = jnp.zeros((main_rows, piece), jnp.float32)
        for j in range(MAIN):
            tail = tail + dot32(
                as_bf16(row == col * MAIN + j), x_all[main_rows:, j * piece : (j + 1) * piece]
            )
        y_ref[:, 0, :, main_width:] = tail.reshape(senders, MAIN, piece).astype(jnp.bfloat16)


def experts(x, expert_in, expert_out, halves):
    senders, groups, _, width = x.shape
    main_rows = senders * MAIN
    feature_dim, hidden_width = expert_in.shape[1], expert_out.shape[1]
    main_width, piece = piece_widths(feature_dim)
    rows = main_rows + main_rows // MAIN
    block = math.gcd(hidden_width, 768 if rows <= 512 else 128)
    steps = hidden_width // block
    slices = groups * halves
    return pl.pallas_call(
        lambda *refs: expert_kernel(feature_dim, *refs),
        grid=(groups, halves, steps),
        out_shape=jax.ShapeDtypeStruct(x.shape, jnp.bfloat16),
        in_specs=[
            pl.BlockSpec((senders, 1, MAIN, width), lambda g, j, f: (0, g, 0, 0)),
            pl.BlockSpec((1, feature_dim, block), lambda g, j, f: (g * halves + j, 0, f)),
            pl.BlockSpec((1, feature_dim, block), lambda g, j, f: (g * halves + j, 0, steps + f)),
            pl.BlockSpec((1, feature_dim, block), lambda g, j, f: (g * halves + j, 0, f)),
        ],
        out_specs=pl.BlockSpec((senders, 1, MAIN, width), lambda g, j, f: (0, g, 0, 0)),
        scratch_shapes=[
            pltpu.VMEM((rows, MAIN * piece), jnp.bfloat16),
            pltpu.VMEM((rows, feature_dim), jnp.float32),
        ],
        compiler_params=pltpu.CompilerParams(
            vmem_limit_bytes=FULL_VMEM, dimension_semantics=("arbitrary",) * 3
        ),
        cost_estimate=pl.CostEstimate(
            flops=6 * rows * feature_dim * hidden_width * slices,
            bytes_accessed=6 * feature_dim * hidden_width * slices,
            transcendentals=rows * hidden_width * slices,
        ),
    )(x, expert_in, expert_in, jnp.swapaxes(expert_out, 1, 2))


def combine_kernel(start_ref, back_ref, code_ref, weight_ref, out_ref):
    feature_dim = out_ref.shape[1]
    main_width, piece = piece_widths(feature_dim)
    senders, groups = back_ref.shape[:2]
    rows = senders * MAIN
    picks = []
    for group in range(groups):
        codes = code_ref[group]
        slot = lax.broadcasted_iota(jnp.int32, codes.shape, 1) % MAIN
        weights = weight_ref[group]
        high = weights.astype(jnp.bfloat16).astype(jnp.float32)
        picks.append((codes, slot, (high, weights - high)))

    def pick(group, chosen):
        codes, slot, parts = picks[group]
        condition = (codes == slot) if chosen is None else (codes == MAIN) & (slot == chosen)
        return [jnp.where(condition, part, 0.0).astype(jnp.bfloat16) for part in parts]

    main = [pick(group, None) for group in range(groups)]
    for j in range(MAIN):
        first, end = j * piece, min((j + 1) * piece, feature_dim)
        value = 0.0 if start_ref is None else start_ref[:, first:end]
        for group in range(groups):
            ninth = pick(group, j)
            tail = back_ref[:, group, :, main_width : main_width + end - first].reshape(rows, -1)
            part = back_ref[:, group, :, first:end].reshape(rows, -1)
            for k in range(2):
                value = value + dot32(main[group][k], part)
                value = value + dot32(ninth[k], tail)
        out_ref[:, first:end] = value.astype(out_ref.dtype)


def combine(start, back, codes, weights, feature_dim):
    alone = start is None
    given = (back, codes, weights) if alone else (start, back, codes, weights)
    return pl.pallas_call(
        (lambda *refs: combine_kernel(None, *refs)) if alone else combine_kernel,
        out_shape=jax.ShapeDtypeStruct(
            (codes.shape[1], feature_dim), jnp.bfloat16 if alone else jnp.float32
        ),
        in_specs=[whole_spec()] * len(given),
        out_specs=whole_spec(),
        compiler_params=pltpu.CompilerParams(vmem_limit_bytes=FULL_VMEM),
    )(*given)


def final_kernel(near_ref, far_ref, out_ref):
    out_ref[...] = (near_ref[...] + far_ref[...].astype(jnp.float32)).T.astype(out_ref.dtype)


def final_sum(near, far):
    rows, feature_dim = near.shape
    return pl.pallas_call(
        final_kernel,
        out_shape=jax.ShapeDtypeStruct((feature_dim, rows), jnp.bfloat16),
        in_specs=[whole_spec()] * 2,
        out_specs=whole_spec(),
        compiler_params=pltpu.CompilerParams(vmem_limit_bytes=FULL_VMEM),
    )(near, far).T


def mirrored(value):
    count = lax.axis_size("col")
    return lax.ppermute(value, "col", [(at, (at + count // 2) % count) for at in range(count)])


def exchange(value):
    rows, cols = lax.axis_size("row"), lax.axis_size("col")
    near = cols // 2
    halves = [
        [row * cols + side * near + at for row in range(rows) for at in range(near)]
        for side in (0, 1)
    ]
    return lax.all_to_all(
        value, ("row", "col"), split_axis=0, concat_axis=0, axis_index_groups=halves, tiled=True
    )


def shards(
    tokens,
    seg_ids,
    norm_gain,
    query_weight,
    kv_weight,
    out_weight,
    sinks,
    moe_gain,
    routes,
    route_weights,
    expert_in,
    expert_out,
):
    own_rows, feature_dim = tokens.shape
    row_count, col_count = lax.axis_size("row"), lax.axis_size("col")
    device_count = row_count * col_count
    row_at, col_at = lax.axis_index("row"), lax.axis_index("col")
    query_cols, kv_cols = query_weight.shape[1], kv_weight.shape[1]

    proj_weight = lax.all_gather(
        jnp.concatenate([query_weight, kv_weight], axis=1), "col", axis=0, tiled=True
    )
    out_cols = out_weight.shape[1]
    cut = up_to(2 * out_cols // 3, 8)
    out_parts = [
        lax.all_gather(part, "col", axis=1, tiled=True)
        for part in (out_weight[:, :cut], out_weight[:, cut:])
    ]

    normed = rms_scale(tokens, norm_gain).astype(jnp.bfloat16)
    block_x = jnp.zeros((row_count, own_rows, feature_dim), jnp.bfloat16)
    for distance in range(row_count):
        piece = swap_rows(normed, distance) if distance else normed
        block_x = lax.dynamic_update_index_in_dim(block_x, piece, row_at ^ distance, 0)
    block_rows = row_count * own_rows
    block_x = block_x.reshape(block_rows, feature_dim)

    all_segs = lax.all_to_all(
        jnp.broadcast_to(seg_ids[None, :], (device_count, own_rows)),
        ("col", "row"),
        split_axis=0,
        concat_axis=0,
        tiled=True,
    ).reshape(-1)
    base_index = col_at * block_rows
    padded_segs = jnp.concatenate([jnp.full((WIN,), -1, jnp.int32), all_segs])
    key_seg = lax.dynamic_slice_in_dim(padded_segs, base_index, WIN + block_rows, 0)
    block_seg = key_seg[WIN:]
    token_index = base_index + jnp.arange(block_rows, dtype=jnp.int32)
    starts = jnp.sum((all_segs[None, :] < block_seg[:, None]).astype(jnp.int32), axis=1)
    positions = token_index - starts

    slices_here = expert_in.shape[0]
    groups = max(1, slices_here // 2)
    halves = min(2, slices_here)
    near_cols = col_count // 2
    members = jnp.arange(row_count * near_cols, dtype=jnp.int32)
    member_at = (
        members // near_cols * col_count + members % near_cols + col_at // near_cols * near_cols
    )

    def slots(route_ids, weights_in):
        expert_ids = jnp.arange(EXPERTS, dtype=jnp.int32)
        named = route_ids[:, :, None] == expert_ids[None, None, :]
        hits = jnp.sum(named.astype(jnp.float32), axis=1)
        expert_weight = jnp.sum(jnp.where(named, weights_in[:, :, None], 0.0), axis=1)
        ranks = jnp.cumsum(hits, axis=0) - hits
        ranks = jnp.where(hits > 0, ranks, -1.0).astype(jnp.int32)
        code_in, code_out, weight_out = [], [], []
        for group in range(groups):
            chosen = member_at * slices_here // 2 + group
            spread = jnp.repeat(ranks[:, chosen], MAIN, axis=1)
            code_out.append(spread)
            code_in.append(spread.T)
            weight_out.append(jnp.repeat(expert_weight[:, chosen], MAIN, axis=1))
        return jnp.stack(code_in), jnp.stack(code_out), jnp.stack(weight_out)

    own_in, own_out, own_weight = slots(routes, route_weights)
    far_in, far_out, far_weight = slots(mirrored(routes), mirrored(route_weights))

    proj_weight, *codes = lax.optimization_barrier(
        (proj_weight, own_in, own_out, own_weight, far_in, far_out, far_weight)
    )
    own_in, own_out, own_weight, far_in, far_out, far_weight = codes
    proj_sum = dot32(block_x, proj_weight)
    query_sum, kv_sum = proj_sum[:, :query_cols], proj_sum[:, query_cols:]
    query_heads = query_cols // HD
    kv_heads = kv_cols // (2 * HD)
    group_size = query_heads // kv_heads
    queries = rotate(query_sum.reshape(block_rows, query_heads, HD), positions).astype(jnp.bfloat16)
    kv_pair = kv_sum.reshape(block_rows, kv_heads, 2, HD)
    keys = rotate(kv_pair[:, :, 0], positions).astype(jnp.bfloat16)
    values = kv_pair[:, :, 1].astype(jnp.bfloat16)
    kv_cache = jnp.stack([keys, values], axis=2).reshape(block_rows, kv_cols)
    edge_kv = from_behind(kv_cache[block_rows - WIN :], "col", 1)
    all_kv = jnp.concatenate([edge_kv, kv_cache], axis=0).reshape(WIN + block_rows, kv_heads, 2, HD)
    key_index = base_index - WIN + jnp.arange(WIN + block_rows, dtype=jnp.int32)
    query_grid = queries.reshape(block_rows, kv_heads, group_size, HD)
    sink_grid = sinks.reshape(kv_heads, group_size)
    attended = attend_tile(
        query_grid,
        all_kv[:, :, 0],
        all_kv[:, :, 1],
        block_seg,
        key_seg,
        token_index,
        key_index,
        sink_grid,
    ).reshape(block_rows, query_cols)

    sums = []
    for part in out_parts:
        if sums:
            part, sums = lax.optimization_barrier((part, sums))
        partial = dot32(attended, part).astype(jnp.bfloat16)
        partial = partial.reshape(row_count, own_rows, part.shape[1])
        pieces = []
        for distance in range(row_count):
            piece = lax.dynamic_index_in_dim(partial, row_at ^ distance, 0, False)
            pieces.append(swap_rows(piece, distance) if distance else piece)
        sums.append(pieces)

    hidden, moe_in = hidden_and_norm(
        tokens, moe_gain.reshape(1, feature_dim), sums, (cut, out_cols - cut)
    )
    far_rows = mirrored(moe_in)
    own_came = exchange(pack(moe_in, own_in))
    far_rows, own_came = lax.optimization_barrier((far_rows, own_came))
    far_came = exchange(pack(far_rows, far_in))
    own_made = experts(own_came, expert_in, expert_out, halves)
    far_came, own_made = lax.optimization_barrier((far_came, own_made))
    own_back = exchange(own_made)
    far_made = experts(far_came, expert_in, expert_out, halves)
    far_made, own_back = lax.optimization_barrier((far_made, own_back))
    far_back = exchange(far_made)
    near_sum = combine(hidden, own_back, own_out, own_weight, feature_dim)
    far_sum = mirrored(combine(None, far_back, far_out, far_weight, feature_dim))
    return (final_sum(near_sum, far_sum), kv_cache)


def solution(mesh):
    in_specs = (
        P(("col", "row"), None),
        P(("col", "row")),
        P(),
        P("col", "row"),
        P("col", "row"),
        P("row", "col"),
        P("row"),
        P(),
        P(("col", "row"), None),
        P(("col", "row"), None),
        P(("row", "col"), None, None),
        P(("row", "col"), None, None),
    )
    out_specs = (P(("col", "row"), None), P("col", "row"))
    return jax.shard_map(shards, mesh=mesh, in_specs=in_specs, out_specs=out_specs, check_vma=False)
```

profile of v0, /device:TPU:0, one launch (start us, length us, event | category | flops | bytes accessed | tf_op | source)
XLA Modules:
  0.0 372.4 jit_solution(8172773199303909586)
XLA Ops:
  20.5 6.1 %all-to-all-start = ((s32[32,1,128]{2,1,0:T(1,128)}), s32[32,1,128]{2,1,0:T(1,128)S(1)}, u32[]{:S(2)}, u32[]{:S(2)}) async-start(s32[32,1,128]{2,1,0:T(1,128)} %broadcast_in_dim.132), calls=%async_computation | async-start | bytes 32768 | tf_op jit(solution)/shard_map/all_to_all | solution.py:388
  41.4 8.1 %all-to-all-done = s32[32,1,128]{2,1,0:T(1,128)S(1)} async-done(((s32[32,1,128]{2,1,0:T(1,128)}), s32[32,1,128]{2,1,0:T(1,128)S(1)}, u32[]{:S(2)}, u32[]{:S(2)}) %all-to-all-start) | async-done | bytes 16416 | tf_op jit(solution)/shard_map/all_to_all | solution.py:388
  59.7 26.8 %all-gather.6.cloned.1.call-done = bf16[2880,1280]{1,0:T(8,128)(2,1)} async-done(((bf16[360,1280]{1,0:T(8,128)(2,1)}), bf16[2880,1280]{1,0:T(8,128)(2,1)}) %all-gather.6.cloned.1.call-update) | async-done | bytes 7372816 | tf_op jit(solution)/shard_map/all_gather | solution.py:370
  86.5 8.2 %fusion.25 = f32[512,1280]{1,0:T(8,128)S(1)} fusion(bf16[512,2880]{1,0:T(8,128)(2,1)} %bitcast.4, bf16[2880,1280]{1,0:T(8,128)(2,1)} %all-gather.6.cloned.1.call-done), kind=kOutput, calls=%fused_computation.116 | convolution fusion | flops 3774873600 | bytes 12943360 | tf_op jit(solution)/shard_map/dot_general | solution.py:98
  108.8 3.2 fusion.1
  112.1 4.5 %fusion = f32[2,8,512]{2,1,0:T(8,128)S(1)} fusion(f32[2,640,512,8]{2,1,3,0:T(8,128)S(1)} %get-tuple-element.77, f32[2,8,512]{2,1,0:T(8,128)S(1)} %broadcast_maximum_fusion, pred[512,640]{0,1:T(8,128)(4,1)S(1)} %fusion.9), kind=kLoop, calls=%fused_computation.11 | loop fusion | flops 20963328 | bytes 21364736 | tf_op jit(solution)/shard_map/reduce_sum | solution.py:72
  116.7 5.9 %fusion.3 = bf16[2,64,8,512]{3,1,2,0:T(8,128)(2,1)S(1)} fusion(f32[2,640,512,8]{2,1,3,0:T(8,128)S(1)} %get-tuple-element.77, f32[2,8,512]{2,1,0:T(8,128)S(1)} %exponential_add_fusion, f32[2,8,512]{2,1,0:T(8,128)S(1)} %broadcast_maximum_fusion, pred[512,640]{0,1:T(8,128)(4,1)S(1)} %fusion.9, bf16[640,2,2,64]{0,3,1,2:T(8,128)(2,1)S(1)} %maximum_maximum_fusion), kind=kOutput, calls=%fused_computation.20 | convolution fusion | flops 697827328 | bytes 22577152 | tf_op jit(solution)/shard_map/kgql,lkd->qkgd/dot_general | solution.py:74
  122.6 8.8 %all-gather.8.cloned.1.call-done = bf16[1024,1920]{0,1:T(8,128)(2,1)} async-done(((bf16[1024,240]{0,1:T(8,128)(2,1)}), bf16[1024,1920]{0,1:T(8,128)(2,1)}) %all-gather.8.cloned.1.call-update) | async-done | bytes 3932176 | tf_op jit(solution)/shard_map/all_gather | solution.py:376
  131.4 4.5 %convolution_convert_fusion = bf16[512,1920]{1,0:T(8,128)(2,1)S(1)} fusion(bf16[512,1024]{0,1:T(8,128)(2,1)S(1)} %bitcast.148, bf16[1024,1920]{0,1:T(8,128)(2,1)} %all-gather.8.cloned.1.call-done), kind=kOutput, calls=%fused_computation.15 | convolution fusion | flops 2014248960 | bytes 6946816 | tf_op jit(solution)/shard_map/dot_general | solution.py:98
  140.6 20.6 %all-gather.4.cloned.1.call-done = bf16[1024,960]{0,1:T(8,128)(2,1)} async-done(((bf16[1024,120]{0,1:T(8,128)(2,1)}), bf16[1024,960]{0,1:T(8,128)(2,1)}) %all-gather.4.cloned.1.call-update) | async-done | bytes 1966096 | tf_op jit(solution)/shard_map/all_gather | solution.py:376
  172.8 8.1 %collective-permute-done.10.refs_8_ = bf16[128,960]{1,0:T(8,128)(2,1)S(1)} collective-permute-done((bf16[128,960]{1,0:T(8,128)(2,1)S(1)}, bf16[128,960]{1,0:T(8,128)(2,1)S(1)}, u32[]{:S(2)}, u32[]{:S(2)}) %collective-permute-start.10) | collective-permute-done | bytes 245792 | tf_op jit(solution)/shard_map/ppermute | solution.py:90
  182.8 4.1 %shard_map.131 = (f32[128,2880]{1,0:T(8,128)}, bf16[128,2880]{1,0:T(8,128)(2,1)}) custom-call(bf16[128,2880]{1,0:T(8,128)(2,1)} %copy.185.refs_0_, f32[1,2880]{1,0:T(1,128)} %reshape.385.refs_1_, bf16[128,1920]{1,0:T(8,128)(2,1)} %get-tuple-element.23.refs_2_, bf16[128,1920]{1,0:T(8,128)(2,1)} %copy-done.9, bf16[128,1920]{1,0:T(8,128)(2,1)} %copy-done.10, ...), custom_call_target="tpu_custom_call" | custom-call | tf_op jit(solution)/shard_map/pallas_call | solution.py:133
  186.9 3.4 shard_map.132
  190.3 4.7 %all-to-all-start.1 = ((bf16[16,2,8,3328]{3,2,1,0:T(8,128)(2,1)}), bf16[16,2,8,3328]{3,2,1,0:T(8,128)(2,1)S(1)}, u32[]{:S(2)}, u32[]{:S(2)}) async-start(bf16[16,2,8,3328]{3,2,1,0:T(8,128)(2,1)} %shard_map.132), calls=%async_computation.1 | async-start | bytes 3407872 | tf_op jit(solution)/shard_map/all_to_all | solution.py:345
  197.2 35.1 %collective-permute-done.12 = bf16[128,2880]{0,1:T(8,128)(2,1)S(1)} collective-permute-done((bf16[128,2880]{0,1:T(8,128)(2,1)}, bf16[128,2880]{0,1:T(8,128)(2,1)S(1)}, u32[]{:S(2)}, u32[]{:S(2)}) %collective-permute-start.12) | collective-permute-done | bytes 737312 | tf_op jit(solution)/shard_map/ppermute | solution.py:335
  235.5 3.3 shard_map.133
  238.8 4.4 %all-to-all-start.2 = ((bf16[16,2,8,3328]{3,2,1,0:T(8,128)(2,1)}), bf16[16,2,8,3328]{3,2,1,0:T(8,128)(2,1)}, u32[]{:S(2)}, u32[]{:S(2)}) async-start(bf16[16,2,8,3328]{3,2,1,0:T(8,128)(2,1)} %shard_map.133), calls=%async_computation.2 | async-start | bytes 3407872 | tf_op jit(solution)/shard_map/all_to_all | solution.py:345
  243.2 22.4 %shard_map.134 = bf16[16,2,8,3328]{3,2,1,0:T(8,128)(2,1)} custom-call(bf16[16,2,8,3328]{3,2,1,0:T(8,128)(2,1)} %copy-done.2, bf16[4,2880,1536]{2,1,0:T(8,128)(2,1)} %refs_2_.3, bf16[4,2880,1536]{2,1,0:T(8,128)(2,1)} %refs_2_.3, bf16[4,2880,768]{2,1,0:T(8,128)(2,1)} %bitcast.126), custom_call_target="tpu_custom_call" | custom-call | flops 7644119040 | bytes 53084160 | tf_op jit(solution)/shard_map/pallas_call | solution.py:246
  266.7 3.9 %all-to-all-start.3 = ((bf16[16,2,8,3328]{3,2,1,0:T(8,128)(2,1)}), bf16[16,2,8,3328]{3,2,1,0:T(8,128)(2,1)S(1)}, u32[]{:S(2)}, u32[]{:S(2)}) async-start(bf16[16,2,8,3328]{3,2,1,0:T(8,128)(2,1)} %shard_map.134), calls=%async_computation.3 | async-start | bytes 3407872 | tf_op jit(solution)/shard_map/all_to_all | solution.py:345
  270.6 22.4 %shard_map.135 = bf16[16,2,8,3328]{3,2,1,0:T(8,128)(2,1)} custom-call(bf16[16,2,8,3328]{3,2,1,0:T(8,128)(2,1)} %all-to-all-done.2.refs_0_, bf16[4,2880,1536]{2,1,0:T(8,128)(2,1)} %refs_2_.3, bf16[4,2880,1536]{2,1,0:T(8,128)(2,1)} %refs_2_.3, bf16[4,2880,768]{2,1,0:T(8,128)(2,1)} %bitcast.127), custom_call_target="tpu_custom_call" | custom-call | flops 7644119040 | bytes 53084160 | tf_op jit(solution)/shard_map/pallas_call | solution.py:246
  294.1 27.6 %all_to_all.26.refs_0_ = bf16[16,2,8,3328]{3,2,1,0:T(8,128)(2,1)} all-to-all(bf16[16,2,8,3328]{3,2,1,0:T(8,128)(2,1)} %shard_map.135), channel_id=1, replica_groups={{0,1,2,3,8,9,10,11,16,17,18,19,24,25,26,27},{4,5,6,7,12,13,14,15,20,21,..., dimensions={0} | all-to-all | bytes 3407872 | tf_op jit(solution)/shard_map/all_to_all | solution.py:345
  321.7 4.1 %shard_map.137 = bf16[128,2880]{1,0:T(8,128)(2,1)} custom-call(bf16[16,2,8,3328]{3,2,1,0:T(8,128)(2,1)} %all_to_all.26.refs_0_, s32[2,128,128]{2,1,0:T(8,128)} %pad_add_fusion.3.refs_1_, f32[2,128,128]{2,1,0:T(8,128)} %pad_maximum_fusion.3.refs_2_), custom_call_target="tpu_custom_call" | custom-call | tf_op jit(solution)/shard_map/pallas_call | solution.py:307
  329.7 4.8 %shard_map.136.near_ref = f32[128,2880]{1,0:T(8,128)} custom-call(f32[128,2880]{1,0:T(8,128)} %get-tuple-element.28.start_ref, bf16[16,2,8,3328]{3,2,1,0:T(8,128)(2,1)} %copy-done.1, s32[2,128,128]{2,1,0:T(8,128)} %pad_add_fusion.1.code_ref, f32[2,128,128]{2,1,0:T(8,128)} %pad_maximum_fusion.2.weight_ref), custom_call_target="tpu_custom_call" | custom-call | tf_op jit(solution)/shard_map/pallas_call | solution.py:307
  334.5 27.5 %collective-permute-done.13 = bf16[128,2880]{0,1:T(8,128)(2,1)S(1)} collective-permute-done((bf16[128,2880]{0,1:T(8,128)(2,1)S(1)}, bf16[128,2880]{0,1:T(8,128)(2,1)S(1)}, u32[]{:S(2)}, u32[]{:S(2)}) %collective-permute-start.13) | collective-permute-done | bytes 737312 | tf_op jit(solution)/shard_map/ppermute | solution.py:335
  (175 shorter events, 85.3 us)
Async XLA Ops:
  7.2 79.3 %all-gather.6.cloned.1.call-start = ((), (), s32[]{:S(2)}) async-start(), calls=%async_computation.6 | async-start | bytes 8294400 | tf_op jit(solution)/shard_map/all_gather | solution.py:370
  9.6 121.8 %all-gather.8.cloned.1.call-start = ((), (), s32[]{:S(2)}) async-start(), calls=%async_computation.7 | async-start | bytes 4423680 | tf_op jit(solution)/shard_map/all_gather | solution.py:376
  12.3 39.3 %collective-permute-start = (bf16[128,2880]{0,1:T(8,128)(2,1)}, bf16[128,2880]{0,1:T(8,128)(2,1)}, u32[]{:S(2)}, u32[]{:S(2)}) collective-permute-start(bf16[128,2880]{0,1:T(8,128)(2,1)} %fusion.6), channel_id=1, source_target_pairs={{0,8},{8,0},{16,24},{24,16},{1,9},{9,1},{17,25},{25,17},{2,10},{10... | collective-permute-start | bytes 2211848 | tf_op jit(solution)/shard_map/ppermute | solution.py:90
  15.2 37.9 %collective-permute-start.1 = (bf16[128,2880]{0,1:T(8,128)(2,1)}, bf16[128,2880]{0,1:T(8,128)(2,1)}, u32[]{:S(2)}, u32[]{:S(2)}) collective-permute-start(bf16[128,2880]{0,1:T(8,128)(2,1)} %fusion.6), channel_id=1, source_target_pairs={{0,16},{8,24},{16,0},{24,8},{1,17},{9,25},{17,1},{25,9},{2,18},{10... | collective-permute-start | bytes 2211848 | tf_op jit(solution)/shard_map/ppermute | solution.py:90
  16.7 37.8 %collective-permute-start.2 = (bf16[128,2880]{0,1:T(8,128)(2,1)}, bf16[128,2880]{0,1:T(8,128)(2,1)}, u32[]{:S(2)}, u32[]{:S(2)}) collective-permute-start(bf16[128,2880]{0,1:T(8,128)(2,1)} %fusion.6), channel_id=1, source_target_pairs={{0,24},{8,16},{16,8},{24,0},{1,25},{9,17},{17,9},{25,1},{2,26},{10... | collective-permute-start | bytes 2211848 | tf_op jit(solution)/shard_map/ppermute | solution.py:90
  16.7 19.5 %collective-permute-start.3 = (s32[128,4]{0,1:T(4,128)S(1)}, s32[128,4]{0,1:T(4,128)S(1)}, u32[]{:S(2)}, u32[]{:S(2)}) collective-permute-start(s32[128,4]{0,1:T(4,128)S(1)} %copy-done.17), channel_id=1, source_target_pairs={{0,4},{1,5},{2,6},{3,7},{4,0},{5,1},{6,2},{7,3},{8,12},{9,13},{10,... | collective-permute-start | bytes 6152 | tf_op jit(solution)/shard_map/ppermute | solution.py:335
  19.8 16.5 %collective-permute-start.4 = (f32[128,4]{0,1:T(4,128)S(1)}, f32[128,4]{0,1:T(4,128)S(1)}, u32[]{:S(2)}, u32[]{:S(2)}) collective-permute-start(f32[128,4]{0,1:T(4,128)S(1)} %copy-done.18), channel_id=1, source_target_pairs={{0,4},{1,5},{2,6},{3,7},{4,0},{5,1},{6,2},{7,3},{8,12},{9,13},{10,... | collective-permute-start | bytes 6152 | tf_op jit(solution)/shard_map/ppermute | solution.py:335
  20.5 29.0 %all-to-all-start = ((s32[32,1,128]{2,1,0:T(1,128)}), s32[32,1,128]{2,1,0:T(1,128)S(1)}, u32[]{:S(2)}, u32[]{:S(2)}) async-start(s32[32,1,128]{2,1,0:T(1,128)} %broadcast_in_dim.132), calls=%async_computation | async-start | bytes 32768 | tf_op jit(solution)/shard_map/all_to_all | solution.py:388
  26.6 134.6 %all-gather.4.cloned.1.call-start = ((), (), s32[]{:S(2)}) async-start(), calls=%async_computation.5 | async-start | bytes 2211840 | tf_op jit(solution)/shard_map/all_gather | solution.py:376
  50.9 48.0 %copy-start.6 = (f32[512,32]{0,1:T(8,128)}, f32[512,32]{0,1:T(8,128)S(1)}, u32[]{:S(2)}) copy-start(f32[512,32]{0,1:T(8,128)S(1)} %get-tuple-element.75) | copy-start | bytes 196612
  101.1 6.5 %collective-permute-start.5 = (bf16[128,256]{0,1:T(8,128)(2,1)}, bf16[128,256]{0,1:T(8,128)(2,1)}, u32[]{:S(2)}, u32[]{:S(2)}) collective-permute-start(bf16[128,256]{0,1:T(8,128)(2,1)} %bitcast.40), channel_id=1, source_target_pairs={{0,1},{1,2},{2,3},{3,4},{4,5},{5,6},{6,7},{8,9},{9,10},{10,11},{11... | collective-permute-start | bytes 196616 | tf_op jit(solution)/shard_map/ppermute | solution.py:26
  122.6 13.3 %copy-start.21 = (bf16[2,64,8,512]{3,1,2,0:T(8,128)(2,1)}, bf16[2,64,8,512]{3,1,2,0:T(8,128)(2,1)S(1)}, u32[]{:S(2)}) copy-start(bf16[2,64,8,512]{3,1,2,0:T(8,128)(2,1)S(1)} %fusion.3) | copy-start | bytes 3145732
  137.1 24.1 %collective-permute-start.6 = (bf16[128,1920]{1,0:T(8,128)(2,1)}, bf16[128,1920]{1,0:T(8,128)(2,1)S(1)}, u32[]{:S(2)}, u32[]{:S(2)}) collective-permute-start(bf16[128,1920]{1,0:T(8,128)(2,1)} %get-tuple-element.58), channel_id=1, source_target_pairs={{0,8},{8,0},{16,24},{24,16},{1,9},{9,1},{17,25},{25,17},{2,10},{10... | collective-permute-start | bytes 1474568 | tf_op jit(solution)/shard_map/ppermute | solution.py:90
  138.5 22.7 %collective-permute-start.7 = (bf16[128,1920]{1,0:T(8,128)(2,1)S(1)}, bf16[128,1920]{1,0:T(8,128)(2,1)S(1)}, u32[]{:S(2)}, u32[]{:S(2)}) collective-permute-start(bf16[128,1920]{1,0:T(8,128)(2,1)S(1)} %get-tuple-element.57), channel_id=1, source_target_pairs={{0,16},{8,24},{16,0},{24,8},{1,17},{9,25},{17,1},{25,9},{2,18},{10... | collective-permute-start | bytes 1474568 | tf_op jit(solution)/shard_map/ppermute | solution.py:90
  140.0 22.1 %collective-permute-start.8 = (bf16[128,1920]{1,0:T(8,128)(2,1)S(1)}, bf16[128,1920]{1,0:T(8,128)(2,1)S(1)}, u32[]{:S(2)}, u32[]{:S(2)}) collective-permute-start(bf16[128,1920]{1,0:T(8,128)(2,1)S(1)} %get-tuple-element.56), channel_id=1, source_target_pairs={{0,24},{8,16},{16,8},{24,0},{1,25},{9,17},{17,9},{25,1},{2,26},{10... | collective-permute-start | bytes 1474568 | tf_op jit(solution)/shard_map/ppermute | solution.py:90
  167.5 13.4 %collective-permute-start.10 = (bf16[128,960]{1,0:T(8,128)(2,1)S(1)}, bf16[128,960]{1,0:T(8,128)(2,1)S(1)}, u32[]{:S(2)}, u32[]{:S(2)}) collective-permute-start(bf16[128,960]{1,0:T(8,128)(2,1)S(1)} %get-tuple-element.61), channel_id=1, source_target_pairs={{0,16},{8,24},{16,0},{24,8},{1,17},{9,25},{17,1},{25,9},{2,18},{10... | collective-permute-start | bytes 737288 | tf_op jit(solution)/shard_map/ppermute | solution.py:90
  169.1 11.8 %collective-permute-start.11 = (bf16[128,960]{1,0:T(8,128)(2,1)S(1)}, bf16[128,960]{1,0:T(8,128)(2,1)S(1)}, u32[]{:S(2)}, u32[]{:S(2)}) collective-permute-start(bf16[128,960]{1,0:T(8,128)(2,1)S(1)} %get-tuple-element.60), channel_id=1, source_target_pairs={{0,24},{8,16},{16,8},{24,0},{1,25},{9,17},{17,9},{25,1},{2,26},{10... | collective-permute-start | bytes 737288 | tf_op jit(solution)/shard_map/ppermute | solution.py:90
  170.4 11.8 %collective-permute-start.9 = (bf16[128,960]{1,0:T(8,128)(2,1)S(1)}, bf16[128,960]{1,0:T(8,128)(2,1)S(1)}, u32[]{:S(2)}, u32[]{:S(2)}) collective-permute-start(bf16[128,960]{1,0:T(8,128)(2,1)S(1)} %get-tuple-element.62), channel_id=1, source_target_pairs={{0,8},{8,0},{16,24},{24,16},{1,9},{9,1},{17,25},{25,17},{2,10},{10... | collective-permute-start | bytes 737288 | tf_op jit(solution)/shard_map/ppermute | solution.py:90
  190.3 43.8 %all-to-all-start.1 = ((bf16[16,2,8,3328]{3,2,1,0:T(8,128)(2,1)}), bf16[16,2,8,3328]{3,2,1,0:T(8,128)(2,1)S(1)}, u32[]{:S(2)}, u32[]{:S(2)}) async-start(bf16[16,2,8,3328]{3,2,1,0:T(8,128)(2,1)} %shard_map.132), calls=%async_computation.1 | async-start | bytes 3407872 | tf_op jit(solution)/shard_map/all_to_all | solution.py:345
  196.2 36.0 %collective-permute-start.12 = (bf16[128,2880]{0,1:T(8,128)(2,1)}, bf16[128,2880]{0,1:T(8,128)(2,1)S(1)}, u32[]{:S(2)}, u32[]{:S(2)}) collective-permute-start(bf16[128,2880]{0,1:T(8,128)(2,1)} %copy.186), channel_id=1, source_target_pairs={{0,4},{1,5},{2,6},{3,7},{4,0},{5,1},{6,2},{7,3},{8,12},{9,13},{10,... | collective-permute-start | bytes 2211848 | tf_op jit(solution)/shard_map/ppermute | solution.py:335
  238.8 27.9 %all-to-all-start.2 = ((bf16[16,2,8,3328]{3,2,1,0:T(8,128)(2,1)}), bf16[16,2,8,3328]{3,2,1,0:T(8,128)(2,1)}, u32[]{:S(2)}, u32[]{:S(2)}) async-start(bf16[16,2,8,3328]{3,2,1,0:T(8,128)(2,1)} %shard_map.133), calls=%async_computation.2 | async-start | bytes 3407872 | tf_op jit(solution)/shard_map/all_to_all | solution.py:345
  266.7 27.4 %all-to-all-start.3 = ((bf16[16,2,8,3328]{3,2,1,0:T(8,128)(2,1)}), bf16[16,2,8,3328]{3,2,1,0:T(8,128)(2,1)S(1)}, u32[]{:S(2)}, u32[]{:S(2)}) async-start(bf16[16,2,8,3328]{3,2,1,0:T(8,128)(2,1)} %shard_map.134), calls=%async_computation.3 | async-start | bytes 3407872 | tf_op jit(solution)/shard_map/all_to_all | solution.py:345
  294.1 31.7 %copy-start.1 = (bf16[16,2,8,3328]{3,2,1,0:T(8,128)(2,1)}, bf16[16,2,8,3328]{3,2,1,0:T(8,128)(2,1)S(1)}, u32[]{:S(2)}) copy-start(bf16[16,2,8,3328]{3,2,1,0:T(8,128)(2,1)S(1)} %all-to-all-done.3.back_ref) | copy-start | bytes 5111812
  327.3 34.6 %collective-permute-start.13 = (bf16[128,2880]{0,1:T(8,128)(2,1)S(1)}, bf16[128,2880]{0,1:T(8,128)(2,1)S(1)}, u32[]{:S(2)}, u32[]{:S(2)}) collective-permute-start(bf16[128,2880]{0,1:T(8,128)(2,1)S(1)} %copy.188), channel_id=1, source_target_pairs={{0,4},{1,5},{2,6},{3,7},{4,0},{5,1},{6,2},{7,3},{8,12},{9,13},{10,... | collective-permute-start | bytes 2211848 | tf_op jit(solution)/shard_map/ppermute | solution.py:335
  (19 other events, 79.8 us)
Sparse Core Ops, SparseCore 0:
  9.7 76.7 all-gather.5
  88.1 43.2 all-gather.7
  133.7 27.4 all-gather.3
where the time goes:
time: 373 us; the launch traced here: 372 us
  waiting for transfers between devices  141 us (38%)
  Pallas kernels  67.2 us (18%)
  starting transfers between devices  39.1 us (10%)
  local copies, waits for them, and re-layouts  38.2 us (10%)
  blocking collectives  27.6 us (7%)
  matrix products  24.8 us (7%)
  other arithmetic  19.7 us (5%)
  between operations  14.4 us (4%)
    ppermute x4, waiting for transfers between devices, mirrored(): lax.ppermute(value, 'col', [(at, (at + count // 2) % count) for at in ran...  62.5 us
    pallas_call x2, Pallas kernels, experts(): pl.pallas_call(lambda *refs: expert_kernel(feature_dim, *refs), grid=(gro...  44.7 us
    all_gather x2, waiting for transfers between devices, shards(): lax.all_gather(part, 'col', axis=1, tiled=True)  29.5 us
    all_to_all x1, blocking collectives, exchange(): lax.all_to_all(value, ('row', 'col'), split_axis=0, concat_axis=0, axis_i...  27.6 us
    all_gather x1, waiting for transfers between devices, shards(): lax.all_gather(jnp.concatenate([query_weight, kv_weight], axis=1), 'col',...  26.8 us
    dot_general x3, matrix products, dot32(): return jnp.dot(left, right, preferred_element_type=jnp.float32)  15.7 us
    all_to_all x3, starting transfers between devices, exchange(): lax.all_to_all(value, ('row', 'col'), split_axis=0, concat_axis=0, axis_i...  13.1 us
    ppermute x9, starting transfers between devices, swap_rows(): lax.ppermute(value, 'row', [(place, place ^ distance) for place in range(...  11.4 us
  transfers between devices with their start and end apart: 21, of which 12 were waited for; matrix products, arithmetic and copies ran while one was open for 19% of the time, Pallas kernels for 13%

commit v1 on v0

--- a/solution.py
+++ b/solution.py
@@ -474,17 +474,17 @@
         tokens, moe_gain.reshape(1, feature_dim), sums, (cut, out_cols - cut)
     )
     far_rows = mirrored(moe_in)
-    own_came = exchange(pack(moe_in, own_in))
-    far_rows, own_came = lax.optimization_barrier((far_rows, own_came))
     far_came = exchange(pack(far_rows, far_in))
+    own_packed, far_came = lax.optimization_barrier((pack(moe_in, own_in), far_came))
+    own_came = exchange(own_packed)
+    far_made = experts(far_came, expert_in, expert_out, halves)
+    own_came, far_made = lax.optimization_barrier((own_came, far_made))
+    far_back = exchange(far_made)
     own_made = experts(own_came, expert_in, expert_out, halves)
-    far_came, own_made = lax.optimization_barrier((far_came, own_made))
-    own_back = exchange(own_made)
-    far_made = experts(far_came, expert_in, expert_out, halves)
-    far_made, own_back = lax.optimization_barrier((far_made, own_back))
-    far_back = exchange(far_made)
-    near_sum = combine(hidden, own_back, own_out, own_weight, feature_dim)
+    far_back, own_made = lax.optimization_barrier((far_back, own_made))
     far_sum = mirrored(combine(None, far_back, far_out, far_weight, feature_dim))
+    near_sum = combine(hidden, exchange(own_made), own_out, own_weight, feature_dim)
+    far_sum, near_sum = lax.optimization_barrier((far_sum, near_sum))
     return (final_sum(near_sum, far_sum), kv_cache)
 
 

time: 373 us -> 370 us (level)
  blocking collectives: 27.6 us -> 0 us
  waiting for transfers between devices: 141 us -> 155 us
  starting transfers between devices: 39.1 us -> 44.7 us
  local copies, waits for them, and re-layouts: 38.2 us -> 42.8 us
    all_to_all x3 -> x4, waiting for transfers between devices: 4.04 us -> 50.3 us  [exchange(): lax.all_to_all(value, ('row', 'col'), split_axis=0, concat_axis=0, axis_i...]
    ppermute x4, waiting for transfers between devices: 62.5 us -> 31.2 us  [mirrored(): lax.ppermute(value, 'col', [(at, (at + count // 2) % count) for at in ran...]
    all_to_all x1 -> x0, blocking collectives: 27.6 us -> none  [exchange(): lax.all_to_all(value, ('row', 'col'), split_axis=0, concat_axis=0, axis_i...]
    all_to_all x3 -> x4, starting transfers between devices: 13.1 us -> 17 us  [exchange(): lax.all_to_all(value, ('row', 'col'), split_axis=0, concat_axis=0, axis_i...]
  transfers between devices with their start and end apart: 21 -> 22, of which waited for: 12 -> 12; matrix products, arithmetic and copies ran while one was open for 19% -> 19% of each run, Pallas kernels for 13% -> 15%
where the time goes in v1:
time: 370 us; the launch traced here: 369 us
  waiting for transfers between devices  155 us (42%)
  Pallas kernels  67.2 us (18%)
  starting transfers between devices  44.7 us (12%)
  local copies, waits for them, and re-layouts  42.8 us (12%)
  matrix products  24.8 us (7%)
  other arithmetic  19.7 us (5%)
  between operations  14.4 us (4%)
    all_to_all x4, waiting for transfers between devices, exchange(): lax.all_to_all(value, ('row', 'col'), split_axis=0, concat_axis=0, axis_i...  50.3 us
    pallas_call x2, Pallas kernels, experts(): pl.pallas_call(lambda *refs: expert_kernel(feature_dim, *refs), grid=(gro...  44.7 us
    ppermute x4, waiting for transfers between devices, mirrored(): lax.ppermute(value, 'col', [(at, (at + count // 2) % count) for at in ran...  31.2 us
    all_gather x2, waiting for transfers between devices, shards(): lax.all_gather(part, 'col', axis=1, tiled=True)  29.4 us
    all_gather x1, waiting for transfers between devices, shards(): lax.all_gather(jnp.concatenate([query_weight, kv_weight], axis=1), 'col',...  26.8 us
    all_to_all x4, starting transfers between devices, exchange(): lax.all_to_all(value, ('row', 'col'), split_axis=0, concat_axis=0, axis_i...  17 us
    dot_general x3, matrix products, dot32(): return jnp.dot(left, right, preferred_element_type=jnp.float32)  15.7 us
    ppermute x9, starting transfers between devices, swap_rows(): lax.ppermute(value, 'row', [(place, place ^ distance) for place in range(...  11.4 us
  transfers between devices with their start and end apart: 22, of which 12 were waited for; matrix products, arithmetic and copies ran while one was open for 19% of the time, Pallas kernels for 15%

profile of v1, /device:TPU:0, one launch (start us, length us, event | category | flops | bytes accessed | tf_op | source)
XLA Modules:
  0.0 369.0 jit_solution(2199121339594149982)
XLA Ops:
  20.4 6.1 %all-to-all-start = ((s32[32,1,128]{2,1,0:T(1,128)}), s32[32,1,128]{2,1,0:T(1,128)S(1)}, u32[]{:S(2)}, u32[]{:S(2)}) async-start(s32[32,1,128]{2,1,0:T(1,128)} %broadcast_in_dim.132), calls=%async_computation | async-start | bytes 32768 | tf_op jit(solution)/shard_map/all_to_all | solution.py:388
  42.0 7.4 %all-to-all-done = s32[32,1,128]{2,1,0:T(1,128)S(1)} async-done(((s32[32,1,128]{2,1,0:T(1,128)}), s32[32,1,128]{2,1,0:T(1,128)S(1)}, u32[]{:S(2)}, u32[]{:S(2)}) %all-to-all-start) | async-done | bytes 16416 | tf_op jit(solution)/shard_map/all_to_all | solution.py:388
  59.6 26.8 %all-gather.6.cloned.1.call-done = bf16[2880,1280]{1,0:T(8,128)(2,1)} async-done(((bf16[360,1280]{1,0:T(8,128)(2,1)}), bf16[2880,1280]{1,0:T(8,128)(2,1)}) %all-gather.6.cloned.1.call-update) | async-done | bytes 7372816 | tf_op jit(solution)/shard_map/all_gather | solution.py:370
  86.5 8.2 %fusion.25 = f32[512,1280]{1,0:T(8,128)S(1)} fusion(bf16[512,2880]{1,0:T(8,128)(2,1)} %bitcast.4, bf16[2880,1280]{1,0:T(8,128)(2,1)} %all-gather.6.cloned.1.call-done), kind=kOutput, calls=%fused_computation.116 | convolution fusion | flops 3774873600 | bytes 12943360 | tf_op jit(solution)/shard_map/dot_general | solution.py:98
  112.0 4.5 %fusion = f32[2,8,512]{2,1,0:T(8,128)S(1)} fusion(f32[2,640,512,8]{2,1,3,0:T(8,128)S(1)} %get-tuple-element.81, f32[2,8,512]{2,1,0:T(8,128)S(1)} %broadcast_maximum_fusion, pred[512,640]{0,1:T(8,128)(4,1)S(1)} %fusion.9), kind=kLoop, calls=%fused_computation.11 | loop fusion | flops 20963328 | bytes 21364736 | tf_op jit(solution)/shard_map/reduce_sum | solution.py:72
  116.7 5.9 %fusion.3 = bf16[2,64,8,512]{3,1,2,0:T(8,128)(2,1)S(1)} fusion(f32[2,640,512,8]{2,1,3,0:T(8,128)S(1)} %get-tuple-element.81, f32[2,8,512]{2,1,0:T(8,128)S(1)} %exponential_add_fusion, f32[2,8,512]{2,1,0:T(8,128)S(1)} %broadcast_maximum_fusion, pred[512,640]{0,1:T(8,128)(4,1)S(1)} %fusion.9, bf16[640,2,2,64]{0,3,1,2:T(8,128)(2,1)S(1)} %maximum_maximum_fusion), kind=kOutput, calls=%fused_computation.20 | convolution fusion | flops 697827328 | bytes 22577152 | tf_op jit(solution)/shard_map/kgql,lkd->qkgd/dot_general | solution.py:74
  122.6 8.9 %all-gather.8.cloned.1.call-done = bf16[1024,1920]{0,1:T(8,128)(2,1)} async-done(((bf16[1024,240]{0,1:T(8,128)(2,1)}), bf16[1024,1920]{0,1:T(8,128)(2,1)}) %all-gather.8.cloned.1.call-update) | async-done | bytes 3932176 | tf_op jit(solution)/shard_map/all_gather | solution.py:376
  131.4 4.5 %convolution_convert_fusion = bf16[512,1920]{1,0:T(8,128)(2,1)S(1)} fusion(bf16[512,1024]{0,1:T(8,128)(2,1)S(1)} %bitcast.148, bf16[1024,1920]{0,1:T(8,128)(2,1)} %all-gather.8.cloned.1.call-done), kind=kOutput, calls=%fused_computation.15 | convolution fusion | flops 2014248960 | bytes 6946816 | tf_op jit(solution)/shard_map/dot_general | solution.py:98
  140.6 20.6 %all-gather.4.cloned.1.call-done = bf16[1024,960]{0,1:T(8,128)(2,1)} async-done(((bf16[1024,120]{0,1:T(8,128)(2,1)}), bf16[1024,960]{0,1:T(8,128)(2,1)}) %all-gather.4.cloned.1.call-update) | async-done | bytes 1966096 | tf_op jit(solution)/shard_map/all_gather | solution.py:376
  173.2 7.7 %collective-permute-done.10.refs_8_ = bf16[128,960]{1,0:T(8,128)(2,1)S(1)} collective-permute-done((bf16[128,960]{1,0:T(8,128)(2,1)S(1)}, bf16[128,960]{1,0:T(8,128)(2,1)S(1)}, u32[]{:S(2)}, u32[]{:S(2)}) %collective-permute-start.10) | collective-permute-done | bytes 245792 | tf_op jit(solution)/shard_map/ppermute | solution.py:90
  182.9 4.2 %shard_map.131 = (f32[128,2880]{1,0:T(8,128)}, bf16[128,2880]{1,0:T(8,128)(2,1)}) custom-call(bf16[128,2880]{1,0:T(8,128)(2,1)} %copy.185.refs_0_, f32[1,2880]{1,0:T(1,128)} %reshape.385.refs_1_, bf16[128,1920]{1,0:T(8,128)(2,1)} %get-tuple-element.25.refs_2_, bf16[128,1920]{1,0:T(8,128)(2,1)} %copy-done.10, bf16[128,1920]{1,0:T(8,128)(2,1)} %copy-done.11, ...), custom_call_target="tpu_custom_call" | custom-call | tf_op jit(solution)/shard_map/pallas_call | solution.py:133
  190.6 31.2 %collective-permute-done.12 = bf16[128,2880]{0,1:T(8,128)(2,1)S(1)} collective-permute-done((bf16[128,2880]{0,1:T(8,128)(2,1)S(1)}, bf16[128,2880]{0,1:T(8,128)(2,1)S(1)}, u32[]{:S(2)}, u32[]{:S(2)}) %collective-permute-start.12) | collective-permute-done | bytes 737312 | tf_op jit(solution)/shard_map/ppermute | solution.py:335
  222.9 3.3 shard_map.133
  226.2 4.7 %all-to-all-start.1 = ((bf16[16,2,8,3328]{3,2,1,0:T(8,128)(2,1)}), bf16[16,2,8,3328]{3,2,1,0:T(8,128)(2,1)S(1)}, u32[]{:S(2)}, u32[]{:S(2)}) async-start(bf16[16,2,8,3328]{3,2,1,0:T(8,128)(2,1)} %shard_map.133), calls=%async_computation.1 | async-start | bytes 3407872 | tf_op jit(solution)/shard_map/all_to_all | solution.py:345
  230.9 3.4 shard_map.132
  234.2 20.1 %all-to-all-done.1.refs_0_ = bf16[16,2,8,3328]{3,2,1,0:T(8,128)(2,1)S(1)} async-done(((bf16[16,2,8,3328]{3,2,1,0:T(8,128)(2,1)}), bf16[16,2,8,3328]{3,2,1,0:T(8,128)(2,1)S(1)}, u32[]{:S(2)}, u32[]{:S(2)}) %all-to-all-start.1) | async-done | bytes 1703968 | tf_op jit(solution)/shard_map/all_to_all | solution.py:345
  254.4 4.4 %all-to-all-start.2 = ((bf16[16,2,8,3328]{3,2,1,0:T(8,128)(2,1)}), bf16[16,2,8,3328]{3,2,1,0:T(8,128)(2,1)}, u32[]{:S(2)}, u32[]{:S(2)}) async-start(bf16[16,2,8,3328]{3,2,1,0:T(8,128)(2,1)} %shard_map.132), calls=%async_computation.2 | async-start | bytes 3407872 | tf_op jit(solution)/shard_map/all_to_all | solution.py:345
  258.8 22.4 %shard_map.134 = bf16[16,2,8,3328]{3,2,1,0:T(8,128)(2,1)} custom-call(bf16[16,2,8,3328]{3,2,1,0:T(8,128)(2,1)} %copy-done.3, bf16[4,2880,1536]{2,1,0:T(8,128)(2,1)} %refs_2_.3, bf16[4,2880,1536]{2,1,0:T(8,128)(2,1)} %refs_2_.3, bf16[4,2880,768]{2,1,0:T(8,128)(2,1)} %bitcast.126), custom_call_target="tpu_custom_call" | custom-call | flops 7644119040 | bytes 53084160 | tf_op jit(solution)/shard_map/pallas_call | solution.py:246
  282.3 3.9 %all-to-all-start.3 = ((bf16[16,2,8,3328]{3,2,1,0:T(8,128)(2,1)}), bf16[16,2,8,3328]{3,2,1,0:T(8,128)(2,1)S(1)}, u32[]{:S(2)}, u32[]{:S(2)}) async-start(bf16[16,2,8,3328]{3,2,1,0:T(8,128)(2,1)} %shard_map.134), calls=%async_computation.3 | async-start | bytes 3407872 | tf_op jit(solution)/shard_map/all_to_all | solution.py:345
  286.2 22.4 %shard_map.135 = bf16[16,2,8,3328]{3,2,1,0:T(8,128)(2,1)} custom-call(bf16[16,2,8,3328]{3,2,1,0:T(8,128)(2,1)} %all-to-all-done.2.refs_0_, bf16[4,2880,1536]{2,1,0:T(8,128)(2,1)} %refs_2_.3, bf16[4,2880,1536]{2,1,0:T(8,128)(2,1)} %refs_2_.3, bf16[4,2880,768]{2,1,0:T(8,128)(2,1)} %bitcast.127), custom_call_target="tpu_custom_call" | custom-call | flops 7644119040 | bytes 53084160 | tf_op jit(solution)/shard_map/pallas_call | solution.py:246
  310.8 4.0 %all-to-all-start.4 = ((bf16[16,2,8,3328]{3,2,1,0:T(8,128)(2,1)}), bf16[16,2,8,3328]{3,2,1,0:T(8,128)(2,1)S(1)}, u32[]{:S(2)}, u32[]{:S(2)}) async-start(bf16[16,2,8,3328]{3,2,1,0:T(8,128)(2,1)} %shard_map.135), calls=%async_computation.4 | async-start | bytes 3407872 | tf_op jit(solution)/shard_map/all_to_all | solution.py:345
  314.9 4.1 %shard_map.136 = bf16[128,2880]{1,0:T(8,128)(2,1)} custom-call(bf16[16,2,8,3328]{3,2,1,0:T(8,128)(2,1)} %copy-done.2, s32[2,128,128]{2,1,0:T(8,128)} %pad_add_fusion.3.refs_1_, f32[2,128,128]{2,1,0:T(8,128)} %pad_maximum_fusion.3.refs_2_), custom_call_target="tpu_custom_call" | custom-call | tf_op jit(solution)/shard_map/pallas_call | solution.py:307
  323.4 28.0 %all-to-all-done.4.back_ref = bf16[16,2,8,3328]{3,2,1,0:T(8,128)(2,1)S(1)} async-done(((bf16[16,2,8,3328]{3,2,1,0:T(8,128)(2,1)}), bf16[16,2,8,3328]{3,2,1,0:T(8,128)(2,1)S(1)}, u32[]{:S(2)}, u32[]{:S(2)}) %all-to-all-start.4) | async-done | bytes 1703968 | tf_op jit(solution)/shard_map/all_to_all | solution.py:345
  352.7 4.8 %shard_map.137.near_ref = f32[128,2880]{1,0:T(8,128)} custom-call(f32[128,2880]{1,0:T(8,128)} %get-tuple-element.40.start_ref, bf16[16,2,8,3328]{3,2,1,0:T(8,128)(2,1)} %copy-done.1, s32[2,128,128]{2,1,0:T(8,128)} %pad_add_fusion.1.code_ref, f32[2,128,128]{2,1,0:T(8,128)} %pad_maximum_fusion.2.weight_ref), custom_call_target="tpu_custom_call" | custom-call | tf_op jit(solution)/shard_map/pallas_call | solution.py:307
  (180 shorter events, 93.0 us)
Async XLA Ops:
  7.2 12.6 %copy-start.21 = (s32[128]{0:T(128)S(1)}, s32[128]{0:T(128)}, u32[]{:S(2)}) copy-start(s32[128]{0:T(128)} %param.13) | copy-start | bytes 1540
  7.2 79.2 %all-gather.6.cloned.1.call-start = ((), (), s32[]{:S(2)}) async-start(), calls=%async_computation.6 | async-start | bytes 8294400 | tf_op jit(solution)/shard_map/all_gather | solution.py:370
  9.6 121.9 %all-gather.8.cloned.1.call-start = ((), (), s32[]{:S(2)}) async-start(), calls=%async_computation.7 | async-start | bytes 4423680 | tf_op jit(solution)/shard_map/all_gather | solution.py:376
  12.2 39.3 %collective-permute-start = (bf16[128,2880]{0,1:T(8,128)(2,1)}, bf16[128,2880]{0,1:T(8,128)(2,1)}, u32[]{:S(2)}, u32[]{:S(2)}) collective-permute-start(bf16[128,2880]{0,1:T(8,128)(2,1)} %fusion.6), channel_id=1, source_target_pairs={{0,8},{8,0},{16,24},{24,16},{1,9},{9,1},{17,25},{25,17},{2,10},{10... | collective-permute-start | bytes 2211848 | tf_op jit(solution)/shard_map/ppermute | solution.py:90
  15.2 37.9 %collective-permute-start.1 = (bf16[128,2880]{0,1:T(8,128)(2,1)}, bf16[128,2880]{0,1:T(8,128)(2,1)}, u32[]{:S(2)}, u32[]{:S(2)}) collective-permute-start(bf16[128,2880]{0,1:T(8,128)(2,1)} %fusion.6), channel_id=1, source_target_pairs={{0,16},{8,24},{16,0},{24,8},{1,17},{9,25},{17,1},{25,9},{2,18},{10... | collective-permute-start | bytes 2211848 | tf_op jit(solution)/shard_map/ppermute | solution.py:90
  16.7 37.8 %collective-permute-start.2 = (bf16[128,2880]{0,1:T(8,128)(2,1)}, bf16[128,2880]{0,1:T(8,128)(2,1)}, u32[]{:S(2)}, u32[]{:S(2)}) collective-permute-start(bf16[128,2880]{0,1:T(8,128)(2,1)} %fusion.6), channel_id=1, source_target_pairs={{0,24},{8,16},{16,8},{24,0},{1,25},{9,17},{17,9},{25,1},{2,26},{10... | collective-permute-start | bytes 2211848 | tf_op jit(solution)/shard_map/ppermute | solution.py:90
  16.7 20.2 %collective-permute-start.3 = (s32[128,4]{0,1:T(4,128)S(1)}, s32[128,4]{0,1:T(4,128)S(1)}, u32[]{:S(2)}, u32[]{:S(2)}) collective-permute-start(s32[128,4]{0,1:T(4,128)S(1)} %copy-done.19), channel_id=1, source_target_pairs={{0,4},{1,5},{2,6},{3,7},{4,0},{5,1},{6,2},{7,3},{8,12},{9,13},{10,... | collective-permute-start | bytes 6152 | tf_op jit(solution)/shard_map/ppermute | solution.py:335
  19.8 17.2 %collective-permute-start.4 = (f32[128,4]{0,1:T(4,128)S(1)}, f32[128,4]{0,1:T(4,128)S(1)}, u32[]{:S(2)}, u32[]{:S(2)}) collective-permute-start(f32[128,4]{0,1:T(4,128)S(1)} %copy-done.20), channel_id=1, source_target_pairs={{0,4},{1,5},{2,6},{3,7},{4,0},{5,1},{6,2},{7,3},{8,12},{9,13},{10,... | collective-permute-start | bytes 6152 | tf_op jit(solution)/shard_map/ppermute | solution.py:335
  20.4 29.0 %all-to-all-start = ((s32[32,1,128]{2,1,0:T(1,128)}), s32[32,1,128]{2,1,0:T(1,128)S(1)}, u32[]{:S(2)}, u32[]{:S(2)}) async-start(s32[32,1,128]{2,1,0:T(1,128)} %broadcast_in_dim.132), calls=%async_computation | async-start | bytes 32768 | tf_op jit(solution)/shard_map/all_to_all | solution.py:388
  26.6 134.6 %all-gather.4.cloned.1.call-start = ((), (), s32[]{:S(2)}) async-start(), calls=%async_computation.5 | async-start | bytes 2211840 | tf_op jit(solution)/shard_map/all_gather | solution.py:376
  101.1 6.5 %collective-permute-start.5 = (bf16[128,256]{0,1:T(8,128)(2,1)}, bf16[128,256]{0,1:T(8,128)(2,1)}, u32[]{:S(2)}, u32[]{:S(2)}) collective-permute-start(bf16[128,256]{0,1:T(8,128)(2,1)} %bitcast.40), channel_id=1, source_target_pairs={{0,1},{1,2},{2,3},{3,4},{4,5},{5,6},{6,7},{8,9},{9,10},{10,11},{11... | collective-permute-start | bytes 196616 | tf_op jit(solution)/shard_map/ppermute | solution.py:26
  122.6 13.4 %copy-start.23 = (bf16[2,64,8,512]{3,1,2,0:T(8,128)(2,1)}, bf16[2,64,8,512]{3,1,2,0:T(8,128)(2,1)S(1)}, u32[]{:S(2)}) copy-start(bf16[2,64,8,512]{3,1,2,0:T(8,128)(2,1)S(1)} %fusion.3) | copy-start | bytes 3145732
  137.1 24.1 %collective-permute-start.6 = (bf16[128,1920]{1,0:T(8,128)(2,1)}, bf16[128,1920]{1,0:T(8,128)(2,1)S(1)}, u32[]{:S(2)}, u32[]{:S(2)}) collective-permute-start(bf16[128,1920]{1,0:T(8,128)(2,1)} %get-tuple-element.62), channel_id=1, source_target_pairs={{0,8},{8,0},{16,24},{24,16},{1,9},{9,1},{17,25},{25,17},{2,10},{10... | collective-permute-start | bytes 1474568 | tf_op jit(solution)/shard_map/ppermute | solution.py:90
  138.6 23.8 %collective-permute-start.7 = (bf16[128,1920]{1,0:T(8,128)(2,1)}, bf16[128,1920]{1,0:T(8,128)(2,1)S(1)}, u32[]{:S(2)}, u32[]{:S(2)}) collective-permute-start(bf16[128,1920]{1,0:T(8,128)(2,1)} %get-tuple-element.61), channel_id=1, source_target_pairs={{0,16},{8,24},{16,0},{24,8},{1,17},{9,25},{17,1},{25,9},{2,18},{10... | collective-permute-start | bytes 1474568 | tf_op jit(solution)/shard_map/ppermute | solution.py:90
  140.1 22.4 %collective-permute-start.8 = (bf16[128,1920]{1,0:T(8,128)(2,1)S(1)}, bf16[128,1920]{1,0:T(8,128)(2,1)S(1)}, u32[]{:S(2)}, u32[]{:S(2)}) collective-permute-start(bf16[128,1920]{1,0:T(8,128)(2,1)S(1)} %get-tuple-element.60), channel_id=1, source_target_pairs={{0,24},{8,16},{16,8},{24,0},{1,25},{9,17},{17,9},{25,1},{2,26},{10... | collective-permute-start | bytes 1474568 | tf_op jit(solution)/shard_map/ppermute | solution.py:90
  167.9 13.0 %collective-permute-start.10 = (bf16[128,960]{1,0:T(8,128)(2,1)S(1)}, bf16[128,960]{1,0:T(8,128)(2,1)S(1)}, u32[]{:S(2)}, u32[]{:S(2)}) collective-permute-start(bf16[128,960]{1,0:T(8,128)(2,1)S(1)} %get-tuple-element.65), channel_id=1, source_target_pairs={{0,16},{8,24},{16,0},{24,8},{1,17},{9,25},{17,1},{25,9},{2,18},{10... | collective-permute-start | bytes 737288 | tf_op jit(solution)/shard_map/ppermute | solution.py:90
  169.4 11.5 %collective-permute-start.11 = (bf16[128,960]{1,0:T(8,128)(2,1)S(1)}, bf16[128,960]{1,0:T(8,128)(2,1)S(1)}, u32[]{:S(2)}, u32[]{:S(2)}) collective-permute-start(bf16[128,960]{1,0:T(8,128)(2,1)S(1)} %get-tuple-element.64), channel_id=1, source_target_pairs={{0,24},{8,16},{16,8},{24,0},{1,25},{9,17},{17,9},{25,1},{2,26},{10... | collective-permute-start | bytes 737288 | tf_op jit(solution)/shard_map/ppermute | solution.py:90
  170.4 11.7 %collective-permute-start.9 = (bf16[128,960]{1,0:T(8,128)(2,1)S(1)}, bf16[128,960]{1,0:T(8,128)(2,1)S(1)}, u32[]{:S(2)}, u32[]{:S(2)}) collective-permute-start(bf16[128,960]{1,0:T(8,128)(2,1)S(1)} %get-tuple-element.66), channel_id=1, source_target_pairs={{0,8},{8,0},{16,24},{24,16},{1,9},{9,1},{17,25},{25,17},{2,10},{10... | collective-permute-start | bytes 737288 | tf_op jit(solution)/shard_map/ppermute | solution.py:90
  188.6 33.2 %collective-permute-start.12 = (bf16[128,2880]{0,1:T(8,128)(2,1)S(1)}, bf16[128,2880]{0,1:T(8,128)(2,1)S(1)}, u32[]{:S(2)}, u32[]{:S(2)}) collective-permute-start(bf16[128,2880]{0,1:T(8,128)(2,1)S(1)} %copy.186), channel_id=1, source_target_pairs={{0,4},{1,5},{2,6},{3,7},{4,0},{5,1},{6,2},{7,3},{8,12},{9,13},{10,... | collective-permute-start | bytes 2211848 | tf_op jit(solution)/shard_map/ppermute | solution.py:335
  226.2 28.2 %all-to-all-start.1 = ((bf16[16,2,8,3328]{3,2,1,0:T(8,128)(2,1)}), bf16[16,2,8,3328]{3,2,1,0:T(8,128)(2,1)S(1)}, u32[]{:S(2)}, u32[]{:S(2)}) async-start(bf16[16,2,8,3328]{3,2,1,0:T(8,128)(2,1)} %shard_map.133), calls=%async_computation.1 | async-start | bytes 3407872 | tf_op jit(solution)/shard_map/all_to_all | solution.py:345
  254.4 27.9 %all-to-all-start.2 = ((bf16[16,2,8,3328]{3,2,1,0:T(8,128)(2,1)}), bf16[16,2,8,3328]{3,2,1,0:T(8,128)(2,1)}, u32[]{:S(2)}, u32[]{:S(2)}) async-start(bf16[16,2,8,3328]{3,2,1,0:T(8,128)(2,1)} %shard_map.132), calls=%async_computation.2 | async-start | bytes 3407872 | tf_op jit(solution)/shard_map/all_to_all | solution.py:345
  282.3 27.4 %all-to-all-start.3 = ((bf16[16,2,8,3328]{3,2,1,0:T(8,128)(2,1)}), bf16[16,2,8,3328]{3,2,1,0:T(8,128)(2,1)S(1)}, u32[]{:S(2)}, u32[]{:S(2)}) async-start(bf16[16,2,8,3328]{3,2,1,0:T(8,128)(2,1)} %shard_map.134), calls=%async_computation.3 | async-start | bytes 3407872 | tf_op jit(solution)/shard_map/all_to_all | solution.py:345
  310.8 40.6 %all-to-all-start.4 = ((bf16[16,2,8,3328]{3,2,1,0:T(8,128)(2,1)}), bf16[16,2,8,3328]{3,2,1,0:T(8,128)(2,1)S(1)}, u32[]{:S(2)}, u32[]{:S(2)}) async-start(bf16[16,2,8,3328]{3,2,1,0:T(8,128)(2,1)} %shard_map.135), calls=%async_computation.4 | async-start | bytes 3407872 | tf_op jit(solution)/shard_map/all_to_all | solution.py:345
  320.5 37.0 %collective-permute-start.13 = (bf16[128,2880]{0,1:T(8,128)(2,1)S(1)}, bf16[128,2880]{0,1:T(8,128)(2,1)}, u32[]{:S(2)}, u32[]{:S(2)}) collective-permute-start(bf16[128,2880]{0,1:T(8,128)(2,1)S(1)} %copy.188), channel_id=1, source_target_pairs={{0,4},{1,5},{2,6},{3,7},{4,0},{5,1},{6,2},{7,3},{8,12},{9,13},{10,... | collective-permute-start | bytes 2211848 | tf_op jit(solution)/shard_map/ppermute | solution.py:335
  (22 other events, 67.8 us)
Sparse Core Ops, SparseCore 0:
  9.7 76.7 all-gather.5
  88.1 43.2 all-gather.7
  133.7 27.4 all-gather.3
